TPU v7x, 256 devices: a whole 4x4x8 slice. The times are simulated.
256 devices in a mesh: group: 8 (over z_hi, x), ctx: 32 (over z_lo, y, core).
Axes of the slice: x: 4, y: 4, z: 8 (z_hi: 2, z_lo: 4; z = z_hi * 4 + z_lo), core: 2. Of those that a mesh axis runs over, the one named last changes fastest.
Arguments:
- queries: bfloat16 [65536, 4096], P(('group', 'ctx')), may hold values from -36 to 36
- resp_keys: bfloat16 [65536, 512], P(('group', 'ctx')), may hold values from -6 to 6
- resp_values: bfloat16 [65536, 512], P(('group', 'ctx')), may hold values from -6 to 6
- lengths: int32 [256], P(('group', 'ctx')), may hold values from 1 to 256, 49152 in all
- prefix_keys: bfloat16 [1024, 512], P(('group', 'ctx')), may hold values from -6 to 6
- prefix_values: bfloat16 [1024, 512], P(('group', 'ctx')), may hold values from -6 to 6
Outputs:
- attended: bfloat16 [65536, 4096], P(('group', 'ctx'))
All inputs are finite; a program needn't handle non-finite values. No bound on the sum of `lengths` on one device may be relied on, other than what follows from the above.
Results may differ from a plain program's by a relative error of at most 0.0055.
Values may be sent and summed in bfloat16 or wider, within the bound.
A program may use at most 128 MiB of HBM per device.

v0:
```python
from functools import partial
import math

import jax
import jax.numpy as jnp
from jax import lax
from jax.sharding import PartitionSpec as P

HEADS = 32
KV_HEADS = 4


def score_rows(grouped, key_rows, head_size, score_scale):
    shaped = key_rows.reshape(key_rows.shape[0], KV_HEADS, head_size)
    return (
        jnp.einsum("rkgd,nkd->rkgn", grouped, shaped, preferred_element_type=jnp.float32)
        * score_scale
    )


def mix_values(weights, value_rows, head_size):
    shaped = value_rows.reshape(value_rows.shape[0], KV_HEADS, head_size)
    return jnp.einsum(
        "rkgn,nkd->rkgd", weights.astype(jnp.bfloat16), shaped, preferred_element_type=jnp.float32
    )


def advance_state(current, key_rows, value_rows, grouped, head_size, score_scale):
    row_max, row_sum, weighted = current
    fresh_scores = score_rows(grouped, key_rows, head_size, score_scale)
    new_max = jnp.maximum(row_max, jnp.max(fresh_scores, axis=-1))
    factor = jnp.exp(row_max - new_max)
    weights = jnp.exp(fresh_scores - new_max[..., None])
    new_sum = row_sum * factor + jnp.sum(weights, axis=-1)
    new_weighted = weighted * factor[..., None] + mix_values(weights, value_rows, head_size)
    return (new_max, new_sum, new_weighted)


def sweep(current, key_rows, value_rows, stepper):
    key_count = key_rows.shape[0]
    block_rows = math.gcd(key_count, 512)
    key_blocks = key_rows.reshape(key_count // block_rows, block_rows, key_rows.shape[1])
    value_blocks = value_rows.reshape(key_count // block_rows, block_rows, value_rows.shape[1])

    def one_block(running, block_pair):
        return (stepper(running, block_pair[0], block_pair[1]), None)

    outcome = lax.scan(one_block, current, (key_blocks, value_blocks))
    return outcome[0]


def shards(queries, resp_keys, resp_values, lengths, prefix_keys, prefix_values):
    row_count = queries.shape[0]
    head_size = resp_keys.shape[1] // KV_HEADS
    score_scale = 1.0 / math.sqrt(head_size)
    grouped = queries.reshape(row_count, KV_HEADS, HEADS // KV_HEADS, head_size)
    positions = lax.iota(jnp.int32, row_count)
    causal = positions[None, :] <= positions[:, None]
    own_scores = score_rows(grouped, resp_keys, head_size, score_scale)
    own_scores = jnp.where(causal[:, None, None, :], own_scores, -1e30)
    own_max = jnp.max(own_scores, axis=-1)
    own_weights = jnp.exp(own_scores - own_max[..., None])
    running = (
        own_max,
        jnp.sum(own_weights, axis=-1),
        mix_values(own_weights, resp_values, head_size),
    )
    stepper = partial(advance_state, grouped=grouped, head_size=head_size, score_scale=score_scale)
    doubled = (
        lax.all_gather(prefix_keys, "group", axis=0, tiled=True),
        lax.all_gather(prefix_values, "group", axis=0, tiled=True),
    )
    gathered = (
        lax.all_gather(doubled[0], "ctx", axis=0, tiled=True),
        lax.all_gather(doubled[1], "ctx", axis=0, tiled=True),
    )
    running = sweep(running, gathered[0], gathered[1], stepper)
    row_max, row_sum, weighted = running
    result = weighted / row_sum[..., None]
    live_rows = positions < lengths[0]
    result = jnp.where(live_rows[:, None, None, None], result, 0.0)
    return result.reshape(row_count, queries.shape[1]).astype(jnp.bfloat16)


def solution(mesh):
    in_specs = (
        P(("group", "ctx"), None),
        P(("group", "ctx"), None),
        P(("group", "ctx"), None),
        P(("group", "ctx")),
        P(("group", "ctx"), None),
        P(("group", "ctx"), None),
    )
    out_specs = P(("group", "ctx"), None)
    return jax.shard_map(shards, mesh=mesh, in_specs=in_specs, out_specs=out_specs, check_vma=False)
```

profile of v0, /device:TPU:1, one launch (start us, length us, event | category | flops | bytes accessed | tf_op | source)
XLA Modules:
  0.0 249.6 jit_solution(15628000608397493227)
XLA Ops:
  6.5 0.0 all-gather.5.cloned.1.call-start
  6.5 40.4 %all-gather = bf16[8,4,512]{2,1,0:T(4,128)(2,1)S(1)} all-gather(bf16[1,4,512]{2,1,0:T(4,128)(2,1)} %bitcast.78), channel_id=1, replica_groups=mesh['group'=8,'ctx'=32] {'group'}, dimensions={0}, use_global_device_ids=true | all-gather | bytes 36864 | tf_op jit(solution)/shard_map/all_gather | solution.py:70
  47.0 0.6 reshape.50
  47.6 0.0 all-gather.5.cloned.1.call-update
  47.6 0.0 all-gather.7.cloned.1.call-start
  47.7 37.5 %all-gather.1 = bf16[8,4,512]{2,1,0:T(4,128)(2,1)S(1)} all-gather(bf16[1,4,512]{2,1,0:T(4,128)(2,1)} %bitcast.79), channel_id=1, replica_groups=mesh['group'=8,'ctx'=32] {'group'}, dimensions={0}, use_global_device_ids=true | all-gather | bytes 36864 | tf_op jit(solution)/shard_map/all_gather | solution.py:71
  85.2 0.6 reshape.52
  85.9 0.0 all-gather.7.cloned.1.call-update
  85.9 4.1 %copy.38 = bf16[256,4096]{0,1:T(8,128)(2,1)} copy(bf16[256,4096]{1,0:T(8,128)(2,1)} %param.8) | data formatting | bytes 4194304 | tf_op args[0]
  90.0 1.0 reshape.44
  91.0 1.0 reshape.46
  92.0 3.1 %copy.45 = bf16[256,4,8,128]{3,0,2,1:T(8,128)(2,1)S(1)} copy(bf16[256,4,8,128]{0,3,2,1:T(8,128)(2,1)} %bitcast.71) | data formatting | bytes 4194304 | tf_op jit(solution)/shard_map/while | solution.py:48
  95.1 3.1 %fusion.12 = (f32[256,4,8]{0,2,1:T(8,128)S(1)}, f32[4,256,256,8]{2,1,3,0:T(8,128)S(1)}) fusion(pred[256,256]{0,1:T(8,128)(4,1)S(1)} %iota_compare_fusion, bf16[256,4,8,128]{0,3,2,1:T(8,128)(2,1)} %bitcast.72, bf16[256,4,128,1]{2,1,0,3:T(4,128)(2,1)S(1)} %bitcast.77), kind=kOutput, calls=%fused_computation.18 | convolution fusion | flops 543154176 | bytes 10846208 | tf_op jit(solution)/shard_map/rkgd,nkd->rkgn/dot_general | solution.py:16
  98.2 0.0 copy-start
  98.2 3.2 %copy-done = f32[4,256,256,8]{2,1,3,0:T(8,128)} copy-done((f32[4,256,256,8]{2,1,3,0:T(8,128)}, f32[4,256,256,8]{2,1,3,0:T(8,128)S(1)}, u32[]{:S(2)}) %copy-start) | copy-done | bytes 8388632
  101.4 4.4 %fusion.19 = f32[256,4,8,128]{3,0,2,1:T(8,128)} fusion(f32[4,256,256,8]{2,1,3,0:T(8,128)S(1)} %get-tuple-element.94, f32[256,4,8]{0,2,1:T(8,128)S(1)} %get-tuple-element.151, pred[256,256]{0,1:T(8,128)(4,1)S(1)} %iota_compare_fusion, bf16[256,4,128,1]{2,1,0,3:T(4,128)(2,1)S(1)} %bitcast.76), kind=kOutput, calls=%fused_computation.25 | convolution fusion | flops 545259520 | bytes 12943360 | tf_op jit(solution)/shard_map/rkgn,nkd->rkgd/dot_general | solution.py:23
  105.8 5.4 %copy.43 = f32[256,4,8,128]{0,3,2,1:T(8,128)} copy(f32[256,4,8,128]{3,0,2,1:T(8,128)} %fusion.19) | data formatting | bytes 8388608 | tf_op jit(solution)/shard_map/while | solution.py:48
  111.8 5.2 %fusion.11 = f32[256,4,8]{0,2,1:T(8,128)S(1)} fusion(f32[4,256,256,8]{2,1,3,0:T(8,128)} %copy-done, f32[256,4,8]{0,2,1:T(8,128)S(1)} %get-tuple-element.151, pred[256,256]{0,1:T(8,128)(4,1)S(1)} %iota_compare_fusion), kind=kLoop, calls=%fused_computation.17 | loop fusion | flops 8380416 | bytes 8519680 | tf_op jit(solution)/shard_map/reduce_sum | solution.py:65
  117.0 0.0 all-gather.5.cloned.1.call-done
  117.0 56.7 %all-gather.7.cloned.1.call-done = bf16[1024,512]{1,0:T(8,128)(2,1)} async-done(((bf16[32,512]{1,0:T(8,128)(2,1)}), bf16[1024,512]{1,0:T(8,128)(2,1)}) %all-gather.7.cloned.1.call-update) | async-done | bytes 1048592 | tf_op jit(solution)/shard_map/all_gather | solution.py:75
  173.7 63.5 %while.14 = (s32[]{:T(128)}, f32[256,4,8]{0,2,1:T(8,128)S(1)}, f32[256,4,8]{0,2,1:T(8,128)S(1)}, f32[256,4,8,128]{0,3,2,1:T(8,128)}, bf16[2,512,512]{2,1,0:T(8,1...) while((s32[]{:T(128)}, f32[256,4,8]{0,2,1:T(8,128)S(1)}, ...), condition=%wide.region_5.6_spmd, body=%wide.region_2.5_spmd.sunk | while | flops 2183151616 | bytes 66584664 | solution.py:48
  173.7 2.1 constant_dynamic-slice_fusion.3
  175.8 1.3 copy.72
  177.0 7.1 %bitcast_reduce_fusion.2 = (f32[256,4,8]{0,2,1:T(8,128)S(1)}, f32[4,512,256,8]{2,1,3,0:T(8,128)}) fusion(bf16[512,4,128,1]{0,2,3,1:T(8,128)(2,1)S(1)} %bitcast.70, bf16[256,4,8,128]{3,0,2,1:T(8,128)(2,1)S(1)} %get-tuple-element.171), kind=kOutput, calls=%fused_computation.1.clone.1 | convolution fusion | flops 1082122240 | bytes 19431424 | tf_op jit(solution)/shard_map/while/body/eval_jaxpr/rkgd,nkd->rkgn/dot_general | solution.py:16
  184.1 8.7 %fusion.40 = f32[256,4,8]{0,2,1:T(8,128)S(1)} fusion(f32[4,512,256,8]{2,1,3,0:T(8,128)} %get-tuple-element.146, f32[256,4,8]{0,2,1:T(8,128)S(1)} %max.4), kind=kLoop, calls=%fused_computation.4.clone.1 | loop fusion | flops 12574720 | bytes 16842752 | tf_op jit(solution)/shard_map/while/body/eval_jaxpr/reduce_sum | solution.py:34
  192.9 0.2 copy.73
  193.1 12.4 %bitcast_add_fusion.2 = f32[256,4,8,128]{0,3,2,1:T(8,128)} fusion(f32[256,4,8,128]{0,3,2,1:T(8,128)} %get-tuple-element.161, bf16[512,4,128,1]{0,2,3,1:T(8,128)(2,1)S(1)} %bitcast.69, f32[4,512,256,8]{2,1,3,0:T(8,128)} %get-tuple-element.146, f32[256,4,8]{0,2,1:T(8,128)S(1)} %max.4, f32[256,4,8]{0,2,1:T(8,128)S(1)} %get-tuple-element.149), kind=kOutput, calls=%fused_computation.8.clone.1 | convolution fusion | flops 1088421888 | bytes 25755648 | tf_op jit(solution)/shard_map/while/body/eval_jaxpr/rkgn,nkd->rkgd/dot_general | solution.py:23
  205.5 2.1 constant_dynamic-slice_fusion.3
  207.5 1.3 copy.72
  208.8 7.1 %bitcast_reduce_fusion.2 = (f32[256,4,8]{0,2,1:T(8,128)S(1)}, f32[4,512,256,8]{2,1,3,0:T(8,128)}) fusion(bf16[512,4,128,1]{0,2,3,1:T(8,128)(2,1)S(1)} %bitcast.70, bf16[256,4,8,128]{3,0,2,1:T(8,128)(2,1)S(1)} %get-tuple-element.171), kind=kOutput, calls=%fused_computation.1.clone.1 | convolution fusion | flops 1082122240 | bytes 19431424 | tf_op jit(solution)/shard_map/while/body/eval_jaxpr/rkgd,nkd->rkgn/dot_general | solution.py:16
  215.8 8.7 %fusion.40 = f32[256,4,8]{0,2,1:T(8,128)S(1)} fusion(f32[4,512,256,8]{2,1,3,0:T(8,128)} %get-tuple-element.146, f32[256,4,8]{0,2,1:T(8,128)S(1)} %max.4), kind=kLoop, calls=%fused_computation.4.clone.1 | loop fusion | flops 12574720 | bytes 16842752 | tf_op jit(solution)/shard_map/while/body/eval_jaxpr/reduce_sum | solution.py:34
  224.6 0.2 copy.73
  224.8 12.4 %bitcast_add_fusion.2 = f32[256,4,8,128]{0,3,2,1:T(8,128)} fusion(f32[256,4,8,128]{0,3,2,1:T(8,128)} %get-tuple-element.161, bf16[512,4,128,1]{0,2,3,1:T(8,128)(2,1)S(1)} %bitcast.69, f32[4,512,256,8]{2,1,3,0:T(8,128)} %get-tuple-element.146, f32[256,4,8]{0,2,1:T(8,128)S(1)} %max.4, f32[256,4,8]{0,2,1:T(8,128)S(1)} %get-tuple-element.149), kind=kOutput, calls=%fused_computation.8.clone.1 | convolution fusion | flops 1088421888 | bytes 25755648 | tf_op jit(solution)/shard_map/while/body/eval_jaxpr/rkgn,nkd->rkgd/dot_general | solution.py:23
  237.2 2.7 %select_convert_fusion = bf16[256,4,8,128]{0,3,2,1:T(8,128)(2,1)S(1)} fusion(f32[256,4,8,128]{0,3,2,1:T(8,128)} %get-tuple-element.43, f32[256,4,8]{0,2,1:T(8,128)S(1)} %get-tuple-element.44, pred[256]{0:T(512)(128)(4,1)S(1)} %iota_compare_fusion.1), kind=kLoop, calls=%fused_computation.20 | loop fusion | flops 3145728 | bytes 6324480 | tf_op jit(solution)/shard_map/convert_element_type | solution.py:82
  239.9 2.9 %copy.61 = bf16[256,4096]{1,0:T(8,128)(2,1)} copy(bf16[256,4096]{0,1:T(8,128)(2,1)S(1)} %bitcast.73) | data formatting | bytes 4194304 | tf_op jit(solution)/shard_map/convert_element_type | solution.py:82
  (8 shorter events, 0.1 us)
Async XLA Ops:
  6.5 110.5 %all-gather.5.cloned.1.call-start = ((), (), s32[]{:S(2)}) async-start(), calls=%async_computation | async-start | bytes 1081344 | tf_op jit(solution)/shard_map/all_gather | solution.py:74
  47.6 126.1 %all-gather.7.cloned.1.call-start = ((), (), s32[]{:S(2)}) async-start(), calls=%async_computation.1 | async-start | bytes 1081344 | tf_op jit(solution)/shard_map/all_gather | solution.py:75
  98.2 3.2 %copy-start = (f32[4,256,256,8]{2,1,3,0:T(8,128)}, f32[4,256,256,8]{2,1,3,0:T(8,128)S(1)}, u32[]{:S(2)}) copy-start(f32[4,256,256,8]{2,1,3,0:T(8,128)S(1)} %get-tuple-element.94) | copy-start | bytes 25165828
Sparse Core Ops, SparseCore 0:
  47.8 66.1 all-gather.4
  115.8 57.8 all-gather.6
where the time goes:
time: 250 us
  blocking collectives  78 us (31%)
  waiting for transfers between devices  56.7 us (23%)
  matrix products  46.3 us (19%)
  local copies, waits for them, and re-layouts  28.9 us (12%)
  other arithmetic  25.5 us (10%)
  between operations  14.1 us (6%)
    all_gather x1, waiting for transfers between devices, shards(): lax.all_gather(doubled[1], 'ctx', axis=0, tiled=True)  56.7 us
    all_gather x1, blocking collectives, shards(): lax.all_gather(prefix_keys, 'group', axis=0, tiled=True)  40.4 us
    all_gather x1, blocking collectives, shards(): lax.all_gather(prefix_values, 'group', axis=0, tiled=True)  37.5 us
    dot_general x3, matrix products, mix_values(): jnp.einsum('rkgn,nkd->rkgd', weights.astype(jnp.bfloat16), shaped, prefer...  29.1 us
    reduce_sum x2, other arithmetic, advance_state(): new_sum = row_sum * factor + jnp.sum(weights, axis=-1)  17.5 us
    dot_general x3, matrix products, score_rows(): jnp.einsum('rkgd,nkd->rkgn', grouped, shaped, preferred_element_type=jnp....  17.2 us
    unnamed x5, local copies, waits for them, and re-layouts  8.55 us
    while x2, local copies, waits for them, and re-layouts, sweep(): outcome = lax.scan(one_block, current, (key_blocks, value_blocks))  8.41 us
  transfers between devices with their start and end apart: 2, of which 1 were waited for; matrix products, arithmetic and copies ran while one was open for 11% of the time, Pallas kernels for 0%

commit v1 on v0

v1 whole, which is shorter than its diff:
```python
import math

import jax
import jax.numpy as jnp
from jax import lax
from jax.experimental import pallas as pl
from jax.experimental.pallas import tpu as pltpu
from jax.sharding import PartitionSpec as P

MESH = pl.DeviceIdType.MESH
KV_HEADS = 4
GROUPS = 8
HEAD = 128
ROWS = 256
BASE2_SCALE = math.log2(math.e) / math.sqrt(HEAD)
NT = (((1,), (1,)), ((), ()))
NN = (((1,), (0,)), ((), ()))

Z_OFFSETS = (0, 1, 7, 2, 6, 3, 5, 4)
PLANE_OFFSETS = sorted(
    [(a, b) for a in range(4) for b in range(4)],
    key=lambda ab: min(ab[0], 4 - ab[0]) + min(ab[1], 4 - ab[1]),
)
PLANES = len(Z_OFFSETS)
PEERS = len(PLANE_OFFSETS)

CHUNKS = ((0, 4), (4, 8))


def device(x, y, z, core):
    return ((z // 4) * 4 + x, (z % 4) * 8 + y * 2 + core)


def matmul(a, b, dims):
    return lax.dot_general(a, b, dims, preferred_element_type=jnp.float32)


def head_lanes(index):
    return pl.ds(pl.multiple_of(index * HEAD, HEAD), HEAD)


def attend(h, keys, values, first, last, live, q_ref, out_ref, acc_ref, max_ref):
    ones = jnp.ones((values.shape[0], HEAD), jnp.bfloat16)
    values_and_ones = jnp.concatenate([values, ones], axis=1)

    def scores_of(g):
        return matmul(q_ref[:, head_lanes(h * GROUPS + g)], keys, NT)

    def weigh(g, scores):
        head = h * GROUPS + g
        if first:
            own = keys.shape[0]
            column = lax.broadcasted_iota(jnp.int32, (ROWS, own), 1)
            row = lax.broadcasted_iota(jnp.int32, (ROWS, own), 0)
            scores = jnp.where(column <= row, scores, -1e30)
        top = jnp.max(scores, axis=1, keepdims=True) * BASE2_SCALE
        top = jnp.broadcast_to(top, (ROWS, HEAD))
        factor = None
        if not first:
            before = max_ref[head]
            top = jnp.maximum(before, top)
            factor = jnp.exp2(before - top)
        if not last:
            max_ref[head] = top
        parts = [
            jnp.exp2(scores[:, i : i + HEAD] * BASE2_SCALE - top).astype(jnp.bfloat16)
            for i in range(0, scores.shape[1], HEAD)
        ]
        return jnp.concatenate(parts, axis=1), factor

    def mix(g, weights, factor):
        head = h * GROUPS + g
        total = matmul(weights, values_and_ones, NN)
        if not first:
            total = acc_ref[head] * jnp.concatenate([factor, factor], axis=1) + total
        if not last:
            acc_ref[head] = total
            return
        result = total[:, :HEAD] * (1.0 / total[:, HEAD:])
        position = lax.broadcasted_iota(jnp.int32, (ROWS, HEAD), 0)
        result = jnp.where(position < live, result, 0.0)
        out_ref[:, head_lanes(head)] = result.astype(jnp.bfloat16)

    following = scores_of(0)
    for g in range(GROUPS):
        current = following
        if g + 1 < GROUPS:
            following = scores_of(g + 1)
        mix(g, *weigh(g, current))


def kernel(
    q_hbm, ok_hbm, ov_hbm, len_ref, pk_hbm, pv_hbm, out_hbm,
    q_ref, ok_ref, ov_ref, pk_ref, pv_ref, out_ref, acc_ref, max_ref, plane_ref, kv_ref,
    load_sems, store_sems, z_send, z_recv, plane_send, plane_recv, core_send, core_recv,
):
    group, ctx = lax.axis_index("group"), lax.axis_index("ctx")
    x, z = group % 4, (group // 4) * 4 + ctx // 8
    y, core = (ctx // 2) % 4, ctx % 2
    plane_peers = [device((x + a) % 4, (y + b) % 4, z, core) for a, b in PLANE_OFFSETS]
    z_peers = [device(x, y, (z + off) % 8, core) for off in Z_OFFSETS]
    sibling = device(x, y, z, 1 - core)

    barrier = pltpu.get_barrier_semaphore()
    for peer in plane_peers[1:] + z_peers[1:] + [sibling]:
        pl.semaphore_signal(barrier, inc=1, device_id=peer, device_id_type=MESH)

    loads = [
        pltpu.make_async_copy(src, dst, load_sems.at[i])
        for i, (src, dst) in enumerate(
            [(pk_hbm, pk_ref), (pv_hbm, pv_ref), (ok_hbm, ok_ref), (ov_hbm, ov_ref), (q_hbm, q_ref)]
        )
    ]
    for load in loads:
        load.start()
    loads[0].wait()
    loads[1].wait()
    for h in range(KV_HEADS):
        rows, lanes = slice(4 * h, 4 * h + 4), slice(HEAD * h, HEAD * h + HEAD)
        plane_ref[0, 0, 0, rows] = pk_ref[:, lanes]
        plane_ref[0, 0, 1, rows] = pv_ref[:, lanes]

    def remote(src, dst, send_sem, recv_sem, peer):
        return pltpu.make_async_remote_copy(
            src_ref=src, dst_ref=dst, send_sem=send_sem, recv_sem=recv_sem,
            device_id=peer, device_id_type=MESH,
        )

    z_copies = [
        remote(plane_ref.at[0, 0], plane_ref.at[j, 0], z_send.at[j], z_recv.at[j], z_peers[j])
        for j in range(1, PLANES)
    ]

    def send_plane(j):
        for p in range(1, PEERS):
            remote(
                plane_ref.at[j, 0], plane_ref.at[j, p],
                plane_send.at[j], plane_recv.at[j], plane_peers[p],
            ).start()

    def wait_plane(j, sems):
        whole = plane_ref.at[j, pl.ds(1, PEERS - 1)]
        pltpu.make_async_copy(whole, whole, sems.at[j]).wait()

    def core_copy(j):
        return remote(kv_ref.at[j, 0], kv_ref.at[j, 1], core_send.at[j], core_recv.at[j], sibling)

    def share_plane(j):
        wait_plane(j, plane_recv)
        for i in range(2):
            for a in range(4):
                for h in range(KV_HEADS):
                    kv_ref[j, 0, i, 16 * a : 16 * a + 16, HEAD * h : HEAD * h + HEAD] = jnp.concatenate(
                        [plane_ref[j, 4 * a + b, i, 4 * h : 4 * h + 4] for b in range(4)], axis=0
                    )
        core_copy(j).start()

    live = len_ref[0]
    refs = (live, q_ref, out_ref, acc_ref, max_ref)

    def own(h, carry):
        lanes = head_lanes(h)
        attend(h, ok_ref[:, lanes], ov_ref[:, lanes], True, False, *refs)
        return carry

    pl.semaphore_wait(barrier, PEERS - 1 + PLANES - 1 + 1)
    for copy in z_copies:
        copy.start()
    send_plane(0)
    for load in loads[2:]:
        load.wait()
    lax.fori_loop(0, 3, own, 0)
    for j in (1, 2):
        z_copies[j - 1].wait_recv()
        send_plane(j)
    lax.fori_loop(3, 4, own, 0)
    for j in range(3, PLANES):
        z_copies[j - 1].wait_recv()
        send_plane(j)

    for j in range(*CHUNKS[0]):
        share_plane(j)
    for index, (begin, end) in enumerate(CHUNKS):
        last = index + 1 == len(CHUNKS)
        for j in range(begin, end):
            core_copy(j).wait_recv()

        def prompt(h, carry, begin=begin, end=end, last=last):
            lanes = head_lanes(h)
            count = (end - begin) * 128
            keys = kv_ref[begin:end, :, 0, :, lanes].reshape(count, HEAD)
            values = kv_ref[begin:end, :, 1, :, lanes].reshape(count, HEAD)
            attend(h, keys, values, False, last, *refs)
            if last:
                columns = pl.ds(pl.multiple_of(h * GROUPS * HEAD, GROUPS * HEAD), GROUPS * HEAD)
                pltpu.make_async_copy(
                    out_ref.at[:, columns], out_hbm.at[:, columns], store_sems.at[h]
                ).start()
            else:
                share_plane(end + h)
            return carry

        lax.fori_loop(0, KV_HEADS, prompt, 0)

    for copy in z_copies:
        copy.wait_send()
    for j in range(PLANES):
        wait_plane(j, plane_send)
        core_copy(j).wait_send()
    for h in range(KV_HEADS):
        columns = pl.ds(h * GROUPS * HEAD, GROUPS * HEAD)
        pltpu.make_async_copy(
            out_ref.at[:, columns], out_hbm.at[:, columns], store_sems.at[h]
        ).wait()


def shards(queries, resp_keys, resp_values, lengths, prefix_keys, prefix_values):
    hbm = pl.BlockSpec(memory_space=pl.ANY)
    bf16, f32 = jnp.bfloat16, jnp.float32
    heads = KV_HEADS * GROUPS
    return pl.pallas_call(
        kernel,
        out_shape=jax.ShapeDtypeStruct(queries.shape, bf16),
        in_specs=[hbm, hbm, hbm, pl.BlockSpec(memory_space=pltpu.SMEM), hbm, hbm],
        out_specs=hbm,
        scratch_shapes=[
            pltpu.VMEM(queries.shape, bf16),
            pltpu.VMEM(resp_keys.shape, bf16),
            pltpu.VMEM(resp_values.shape, bf16),
            pltpu.VMEM(prefix_keys.shape, bf16),
            pltpu.VMEM(prefix_values.shape, bf16),
            pltpu.VMEM(queries.shape, bf16),
            pltpu.VMEM((heads, ROWS, 2 * HEAD), f32),
            pltpu.VMEM((heads, ROWS, HEAD), f32),
            pltpu.VMEM((PLANES, PEERS, 2, 16, HEAD), bf16),
            pltpu.VMEM((PLANES, 2, 2, 64, KV_HEADS * HEAD), bf16),
            pltpu.SemaphoreType.DMA((5,)),
            pltpu.SemaphoreType.DMA((KV_HEADS,)),
        ]
        + [pltpu.SemaphoreType.DMA((PLANES,))] * 6,
        compiler_params=pltpu.CompilerParams(
            collective_id=0, has_side_effects=True, vmem_limit_bytes=48 << 20
        ),
        name="attend_and_gather",
    )(queries, resp_keys, resp_values, lengths, prefix_keys, prefix_values)


def solution(mesh):
    rows = P(("group", "ctx"), None)
    in_specs = (rows, rows, rows, P(("group", "ctx")), rows, rows)
    return jax.shard_map(shards, mesh=mesh, in_specs=in_specs, out_specs=rows, check_vma=False)
```

time: 250 us -> 47.1 us (0.19)
  blocking collectives: 78 us -> 0 us
  waiting for transfers between devices: 56.7 us -> 0 us
  matrix products: 46.3 us -> 0 us
  Pallas kernels: 0 us -> 40 us
  other arithmetic: 25.5 us -> 0 us
  local copies, waits for them, and re-layouts: 28.9 us -> 6.18 us
  between operations: 14.1 us -> 0.67 us
    all_gather x2 -> x0, blocking collectives: 78 us -> none  [the longest x1 40.4 us: shards(): lax.all_gather(prefix_keys, 'group', axis=0, tiled=True)]
    all_gather x2 -> x0, waiting for transfers between devices: 56.7 us -> none  [the longest x1 56.7 us: shards(): lax.all_gather(doubled[1], 'ctx', axis=0, tiled=True)]
    dot_general x6 -> x0, matrix products: 46.3 us -> none  [the longest x3 29.1 us: mix_values(): jnp.einsum('rkgn,nkd->rkgd', weights.astype(jnp.bfloat16), shaped, prefer...]
    pallas_call x0 -> x1, Pallas kernels: none -> 40 us  [shards(): pl.pallas_call(kernel, out_shape=jax.ShapeDtypeStruct(queries.shape, bf16...]
    reduce_sum x3 -> x0, other arithmetic: 22.7 us -> none  [the longest x2 17.5 us: advance_state(): new_sum = row_sum * factor + jnp.sum(weights, axis=-1)]
    while x4 -> x0, local copies, waits for them, and re-layouts: 8.42 us -> none  [the longest x2 8.41 us: sweep(): outcome = lax.scan(one_block, current, (key_blocks, value_blocks))]
    dynamic_slice x6 -> x0, local copies, waits for them, and re-layouts: 7.05 us -> none  [sweep(): outcome = lax.scan(one_block, current, (key_blocks, value_blocks))]
    convert_element_type x1 -> x0, local copies, waits for them, and re-layouts: 2.86 us -> none  [shards(): return result.reshape(row_count, queries.shape[1]).astype(jnp.bfloat16)]
  transfers between devices with their start and end apart: 2 -> 0, of which waited for: 1 -> 0; matrix products, arithmetic and copies ran while one was open for 11% -> 0% of each run, Pallas kernels for 0% -> 0%
where the time goes in v1:
time: 47.1 us; the launch traced here: 46.9 us
  Pallas kernels  40 us (85%)
  local copies, waits for them, and re-layouts  6.18 us (13%)
  between operations  0.67 us (1%)
    pallas_call x1, Pallas kernels, shards(): pl.pallas_call(kernel, out_shape=jax.ShapeDtypeStruct(queries.shape, bf16...  40 us
    unnamed x11, local copies, waits for them, and re-layouts  6.18 us

profile of v1, /device:TPU:1, one launch (start us, length us, event | category | flops | bytes accessed | tf_op | source)
XLA Modules:
  0.0 46.9 jit_solution(11908789531382672816)
XLA Ops:
  0.7 0.0 copy-start
  0.7 1.6 %copy-done = bf16[256,4096]{1,0:T(8,128)(2,1)S(1)} copy-done((bf16[256,4096]{1,0:T(8,128)(2,1)S(1)}, bf16[256,4096]{1,0:T(8,128)(2,1)}, u32[]{:S(2)}) %copy-start) | copy-done | bytes 2097176
  2.2 0.0 copy-start.1
  2.2 0.9 %copy-done.1 = bf16[256,512]{1,0:T(8,128)(2,1)S(1)} copy-done((bf16[256,512]{1,0:T(8,128)(2,1)S(1)}, bf16[256,512]{1,0:T(8,128)(2,1)}, u32[]{:S(2)}) %copy-start.1) | copy-done | bytes 262168
  3.2 0.0 copy-start.2
  3.2 0.9 %copy-done.2 = bf16[256,512]{1,0:T(8,128)(2,1)S(1)} copy-done((bf16[256,512]{1,0:T(8,128)(2,1)S(1)}, bf16[256,512]{1,0:T(8,128)(2,1)}, u32[]{:S(2)}) %copy-start.2) | copy-done | bytes 262168
  4.1 0.0 copy-start.3
  4.1 0.7 %copy-done.3 = bf16[4,512]{1,0:T(4,128)(2,1)S(1)} copy-done((bf16[4,512]{1,0:T(4,128)(2,1)S(1)}, bf16[4,512]{1,0:T(4,128)(2,1)}, u32[]{:S(2)}) %copy-start.3) | copy-done | bytes 4120
  4.8 0.0 copy-start.4
  4.8 0.7 %copy-done.4 = bf16[4,512]{1,0:T(4,128)(2,1)S(1)} copy-done((bf16[4,512]{1,0:T(4,128)(2,1)S(1)}, bf16[4,512]{1,0:T(4,128)(2,1)}, u32[]{:S(2)}) %copy-start.4) | copy-done | bytes 4120
  5.5 40.0 %attend_and_gather.1 = bf16[256,4096]{1,0:T(8,128)(2,1)S(1)} custom-call(bf16[256,4096]{1,0:T(8,128)(2,1)S(1)} %copy-done, bf16[256,512]{1,0:T(8,128)(2,1)S(1)} %copy-done.1, bf16[256,512]{1,0:T(8,128)(2,1)S(1)} %copy-done.2, s32[1]{0:T(128)S(6)} %copy.8.len_ref, bf16[4,512]{1,0:T(4,128)(2,1)S(1)} %copy-done.3, bf16[4,512]{1,0:T(4,128)(2,1)S(1)} %copy-done.4), custom_call_target="tpu_custom_call" | custom-call | tf_op jit(solution)/shard_map/attend_and_gather/pallas_call | solution.py:221
  45.5 1.3 %copy.9 = bf16[256,4096]{1,0:T(8,128)(2,1)} copy(bf16[256,4096]{1,0:T(8,128)(2,1)S(1)} %attend_and_gather.1) | data formatting | bytes 4194304
Async XLA Ops:
  0.7 1.6 %copy-start = (bf16[256,4096]{1,0:T(8,128)(2,1)S(1)}, bf16[256,4096]{1,0:T(8,128)(2,1)}, u32[]{:S(2)}) copy-start(bf16[256,4096]{1,0:T(8,128)(2,1)} %q_hbm.1) | copy-start | bytes 6291460
  2.2 0.9 %copy-start.1 = (bf16[256,512]{1,0:T(8,128)(2,1)S(1)}, bf16[256,512]{1,0:T(8,128)(2,1)}, u32[]{:S(2)}) copy-start(bf16[256,512]{1,0:T(8,128)(2,1)} %ok_hbm.1) | copy-start | bytes 786436
  3.2 0.9 %copy-start.2 = (bf16[256,512]{1,0:T(8,128)(2,1)S(1)}, bf16[256,512]{1,0:T(8,128)(2,1)}, u32[]{:S(2)}) copy-start(bf16[256,512]{1,0:T(8,128)(2,1)} %ov_hbm.1) | copy-start | bytes 786436
  4.1 0.7 %copy-start.3 = (bf16[4,512]{1,0:T(4,128)(2,1)S(1)}, bf16[4,512]{1,0:T(4,128)(2,1)}, u32[]{:S(2)}) copy-start(bf16[4,512]{1,0:T(4,128)(2,1)} %pk_hbm.1) | copy-start | bytes 12292
  4.8 0.7 %copy-start.4 = (bf16[4,512]{1,0:T(4,128)(2,1)S(1)}, bf16[4,512]{1,0:T(4,128)(2,1)}, u32[]{:S(2)}) copy-start(bf16[4,512]{1,0:T(4,128)(2,1)} %pv_hbm.1) | copy-start | bytes 12292

commit v2 on v1

v2 whole, which is shorter than its diff:
```python
import math

import jax
import jax.numpy as jnp
from jax import lax
from jax.experimental import pallas as pl
from jax.experimental.pallas import tpu as pltpu
from jax.sharding import PartitionSpec as P

MESH = pl.DeviceIdType.MESH
KV_HEADS = 4
GROUPS = 8
HEAD = 128
ROWS = 256
BASE2_SCALE = math.log2(math.e) / math.sqrt(HEAD)
NT = (((1,), (1,)), ((), ()))
NN = (((1,), (0,)), ((), ()))

Z_OFFSETS = (0, 1, 7, 2, 6, 3, 5, 4)
RING_OFFSETS = (0, 1, 3, 2)
PLANES = len(Z_OFFSETS)
RING = len(RING_OFFSETS)

CHUNKS = ((0, 2), (2, 8))


def device(x, y, z, core):
    return ((z // 4) * 4 + x, (z % 4) * 8 + y * 2 + core)


def matmul(a, b, dims):
    return lax.dot_general(a, b, dims, preferred_element_type=jnp.float32)


def head_lanes(index):
    return pl.ds(pl.multiple_of(index * HEAD, HEAD), HEAD)


def attend(h, keys, values, first, last, len_ref, q_ref, out_ref, acc_ref, max_ref):
    ones = jnp.ones((values.shape[0], HEAD), jnp.bfloat16)
    values_and_ones = jnp.concatenate([values, ones], axis=1)

    def scores_of(g):
        return matmul(q_ref[:, head_lanes(h * GROUPS + g)], keys, NT)

    def weigh(g, scores):
        head = h * GROUPS + g
        if first:
            own = keys.shape[0]
            column = lax.broadcasted_iota(jnp.int32, (ROWS, own), 1)
            row = lax.broadcasted_iota(jnp.int32, (ROWS, own), 0)
            scores = jnp.where(column <= row, scores, -1e30)
        top = jnp.max(scores, axis=1, keepdims=True) * BASE2_SCALE
        top = jnp.broadcast_to(top, (ROWS, HEAD))
        factor = None
        if not first:
            before = max_ref[head]
            top = jnp.maximum(before, top)
            factor = jnp.exp2(before - top)
        if not last:
            max_ref[head] = top
        parts = [
            jnp.exp2(scores[:, i : i + HEAD] * BASE2_SCALE - top).astype(jnp.bfloat16)
            for i in range(0, scores.shape[1], HEAD)
        ]
        return jnp.concatenate(parts, axis=1), factor

    def mix(g, weights, factor):
        head = h * GROUPS + g
        total = matmul(weights, values_and_ones, NN)
        if not first:
            total = acc_ref[head] * jnp.concatenate([factor, factor], axis=1) + total
        if not last:
            acc_ref[head] = total
            return
        result = total[:, :HEAD] * (1.0 / total[:, HEAD:])
        position = lax.broadcasted_iota(jnp.int32, (ROWS, HEAD), 0)
        result = jnp.where(position < len_ref[0], result, 0.0)
        out_ref[:, head_lanes(head)] = result.astype(jnp.bfloat16)

    following = scores_of(0)
    for g in range(GROUPS):
        current = following
        if g + 1 < GROUPS:
            following = scores_of(g + 1)
        mix(g, *weigh(g, current))


def kernel(
    q_hbm, ok_hbm, ov_hbm, len_hbm, pk_hbm, pv_hbm, out_hbm,
    len_ref, q_ref, ok_ref, ov_ref, pk_ref, pv_ref, out_ref, acc_ref, max_ref, part_ref, kv_ref,
    load_sems, store_sems, part_send, part_recv, plane_send, plane_recv, core_send, core_recv,
):
    group, ctx = lax.axis_index("group"), lax.axis_index("ctx")
    x, z = group % 4, (group // 4) * 4 + ctx // 8
    y, core = (ctx // 2) % 4, ctx % 2

    def first_peer(a, j):
        return device(
            (x + RING_OFFSETS[a] * (1 - core)) % 4,
            (y + RING_OFFSETS[a] * core) % 4,
            (z + Z_OFFSETS[j]) % 8,
            core,
        )

    def last_peer(b):
        return device(
            (x + RING_OFFSETS[b] * core) % 4, (y + RING_OFFSETS[b] * (1 - core)) % 4, z, core
        )

    sibling = device(x, y, z, 1 - core)
    first_peers = {(a, j): first_peer(a, j) for j in range(PLANES) for a in range(RING) if a + j}
    last_peers = [last_peer(b) for b in range(RING)]

    barrier = pltpu.get_barrier_semaphore()
    for peer in list(first_peers.values()) + last_peers[1:] + [sibling]:
        pl.semaphore_signal(barrier, inc=1, device_id=peer, device_id_type=MESH)

    loads = [
        pltpu.make_async_copy(src, dst, load_sems.at[i])
        for i, (src, dst) in enumerate(
            [
                (pk_hbm, pk_ref), (pv_hbm, pv_ref), (len_hbm, len_ref),
                (ok_hbm, ok_ref), (ov_hbm, ov_ref), (q_hbm, q_ref),
            ]
        )
    ]
    for load in loads:
        load.start()
    loads[0].wait()
    loads[1].wait()
    for h in range(KV_HEADS):
        rows, lanes = slice(4 * h, 4 * h + 4), slice(HEAD * h, HEAD * h + HEAD)
        part_ref[0, 0, 0, rows] = pk_ref[:, lanes]
        part_ref[0, 0, 1, rows] = pv_ref[:, lanes]

    def remote(src, dst, send_sem, recv_sem, peer):
        return pltpu.make_async_remote_copy(
            src_ref=src, dst_ref=dst, send_sem=send_sem, recv_sem=recv_sem,
            device_id=peer, device_id_type=MESH,
        )

    def send_part():
        for j in range(PLANES):
            for a in range(RING):
                if a + j:
                    remote(
                        part_ref.at[0, 0], part_ref.at[j, a],
                        part_send.at[j], part_recv.at[j], first_peers[a, j],
                    ).start()

    def wait_part(j, sems):
        whole = part_ref.at[j] if j else part_ref.at[0, pl.ds(1, RING - 1)]
        pltpu.make_async_copy(whole, whole, sems.at[j]).wait()

    def send_plane(j):
        wait_part(j, part_recv)
        for i in range(2):
            for h in range(KV_HEADS):
                kv_ref[j, 0, 0, i, :, HEAD * h : HEAD * h + HEAD] = jnp.concatenate(
                    [part_ref[j, a, i, 4 * h : 4 * h + 4] for a in range(RING)], axis=0
                )
        for b in range(1, RING):
            remote(
                kv_ref.at[j, 0, 0], kv_ref.at[j, 0, b],
                plane_send.at[j], plane_recv.at[j], last_peers[b],
            ).start()

    def wait_plane(j, sems):
        whole = kv_ref.at[j, 0, pl.ds(1, RING - 1)]
        pltpu.make_async_copy(whole, whole, sems.at[j]).wait()

    def core_copy(j):
        return remote(kv_ref.at[j, 0], kv_ref.at[j, 1], core_send.at[j], core_recv.at[j], sibling)

    def share_plane(j):
        wait_plane(j, plane_recv)
        core_copy(j).start()

    refs = (len_ref, q_ref, out_ref, acc_ref, max_ref)

    def own(h, carry):
        lanes = head_lanes(h)
        attend(h, ok_ref[:, lanes], ov_ref[:, lanes], True, False, *refs)
        return carry

    pl.semaphore_wait(barrier, len(first_peers) + RING - 1 + 1)
    send_part()
    for load in loads[2:]:
        load.wait()
    lax.fori_loop(0, KV_HEADS, own, 0)
    shared = 0
    for j in range(PLANES):
        send_plane(j)
        if j >= 2 and j % 2 == 0 and shared < CHUNKS[0][1]:
            share_plane(shared)
            shared += 1
    for j in range(shared, CHUNKS[0][1]):
        share_plane(j)
    for index, (begin, end) in enumerate(CHUNKS):
        last = index + 1 == len(CHUNKS)
        coming = 0 if last else CHUNKS[index + 1][1] - end
        for j in range(begin, end):
            core_copy(j).wait_recv()

        def prompt(h, carry, begin=begin, end=end, last=last, coming=coming):
            lanes = head_lanes(h)
            count = (end - begin) * 128
            keys = kv_ref[begin:end, :, :, 0, :, lanes].reshape(count, HEAD)
            values = kv_ref[begin:end, :, :, 1, :, lanes].reshape(count, HEAD)
            attend(h, keys, values, False, last, *refs)
            if last:
                columns = pl.ds(pl.multiple_of(h * GROUPS * HEAD, GROUPS * HEAD), GROUPS * HEAD)
                pltpu.make_async_copy(
                    out_ref.at[:, columns], out_hbm.at[:, columns], store_sems.at[h]
                ).start()
            elif coming >= KV_HEADS:
                share_plane(end + h)
            else:

                @pl.when(h < coming)
                def _():
                    share_plane(end + h)

            return carry

        lax.fori_loop(0, KV_HEADS, prompt, 0)
        for j in range(end + KV_HEADS, end + coming):
            share_plane(j)

    for j in range(PLANES):
        wait_part(j, part_send)
        wait_plane(j, plane_send)
        core_copy(j).wait_send()
    for h in range(KV_HEADS):
        columns = pl.ds(h * GROUPS * HEAD, GROUPS * HEAD)
        pltpu.make_async_copy(
            out_ref.at[:, columns], out_hbm.at[:, columns], store_sems.at[h]
        ).wait()


def shards(queries, resp_keys, resp_values, lengths, prefix_keys, prefix_values):
    hbm = pl.BlockSpec(memory_space=pl.ANY)
    bf16, f32 = jnp.bfloat16, jnp.float32
    heads = KV_HEADS * GROUPS
    return pl.pallas_call(
        kernel,
        out_shape=pltpu.VMEM(queries.shape, bf16),
        in_specs=[hbm] * 6,
        out_specs=hbm,
        scratch_shapes=[
            pltpu.SMEM(lengths.shape, jnp.int32),
            pltpu.VMEM(queries.shape, bf16),
            pltpu.VMEM(resp_keys.shape, bf16),
            pltpu.VMEM(resp_values.shape, bf16),
            pltpu.VMEM(prefix_keys.shape, bf16),
            pltpu.VMEM(prefix_values.shape, bf16),
            pltpu.VMEM(queries.shape, bf16),
            pltpu.VMEM((heads, ROWS, 2 * HEAD), f32),
            pltpu.VMEM((heads, ROWS, HEAD), f32),
            pltpu.VMEM((PLANES, RING, 2, 16, HEAD), bf16),
            pltpu.VMEM((PLANES, 2, RING, 2, 16, KV_HEADS * HEAD), bf16),
            pltpu.SemaphoreType.DMA((6,)),
            pltpu.SemaphoreType.DMA((KV_HEADS,)),
        ]
        + [pltpu.SemaphoreType.DMA((PLANES,))] * 6,
        compiler_params=pltpu.CompilerParams(
            collective_id=0, has_side_effects=True, vmem_limit_bytes=58 << 20
        ),
        name="attend_and_gather",
    )(queries, resp_keys, resp_values, lengths, prefix_keys, prefix_values)


def solution(mesh):
    rows = P(("group", "ctx"), None)
    in_specs = (rows, rows, rows, P(("group", "ctx")), rows, rows)
    return jax.shard_map(shards, mesh=mesh, in_specs=in_specs, out_specs=rows, check_vma=False)
```

time: 47.1 us -> 40.9 us (0.87)
  local copies, waits for them, and re-layouts: 6.18 us -> 1.32 us
  Pallas kernels: 40 us -> 38.8 us
    unnamed x11 -> x1, local copies, waits for them, and re-layouts: 6.18 us -> 1.32 us
    pallas_call x1, Pallas kernels: 40 us -> 38.8 us  [shards(): pl.pallas_call(kernel, out_shape=pltpu.VMEM(queries.shape, bf16), in_spec...]
where the time goes in v2:
time: 40.9 us; the launch traced here: 40.8 us
  Pallas kernels  38.8 us (95%)
  local copies, waits for them, and re-layouts  1.32 us (3%)
  between operations  0.66 us (2%)
    pallas_call x1, Pallas kernels, shards(): pl.pallas_call(kernel, out_shape=pltpu.VMEM(queries.shape, bf16), in_spec...  38.8 us
    unnamed x1, local copies, waits for them, and re-layouts  1.32 us

profile of v2, /device:TPU:1, one launch (start us, length us, event | category | flops | bytes accessed | tf_op | source)
XLA Modules:
  0.0 40.8 jit_solution(3558476829309951254)
XLA Ops:
  0.7 38.8 %attend_and_gather.1 = bf16[256,4096]{1,0:T(8,128)(2,1)S(1)} custom-call(bf16[256,4096]{1,0:T(8,128)(2,1)} %q_hbm.1, bf16[256,512]{1,0:T(8,128)(2,1)} %ok_hbm.1, bf16[256,512]{1,0:T(8,128)(2,1)} %ov_hbm.1, s32[1]{0:T(128)S(6)} %copy.9.len_hbm, bf16[4,512]{1,0:T(4,128)(2,1)} %pk_hbm.1, bf16[4,512]{1,0:T(4,128)(2,1)} %pv_hbm.1), custom_call_target="tpu_custom_call" | custom-call | tf_op jit(solution)/shard_map/attend_and_gather/pallas_call | solution.py:246
  39.5 1.3 %copy.8 = bf16[256,4096]{1,0:T(8,128)(2,1)} copy(bf16[256,4096]{1,0:T(8,128)(2,1)S(1)} %attend_and_gather.1) | data formatting | bytes 4194304

commit v3 on v2

--- a/solution.py
+++ b/solution.py
@@ -87,9 +87,9 @@
 
 
 def kernel(
-    q_hbm, ok_hbm, ov_hbm, len_hbm, pk_hbm, pv_hbm, out_hbm,
-    len_ref, q_ref, ok_ref, ov_ref, pk_ref, pv_ref, out_ref, acc_ref, max_ref, part_ref, kv_ref,
-    load_sems, store_sems, part_send, part_recv, plane_send, plane_recv, core_send, core_recv,
+    q_hbm, ok_hbm, ov_hbm, len_hbm, pk_hbm, pv_hbm, out_ref,
+    len_ref, q_ref, ok_ref, ov_ref, pk_ref, pv_ref, acc_ref, max_ref, part_ref, kv_ref,
+    load_sems, part_send, part_recv, plane_send, plane_recv, core_send, core_recv,
 ):
     group, ctx = lax.axis_index("group"), lax.axis_index("ctx")
     x, z = group % 4, (group // 4) * 4 + ctx // 8
@@ -188,9 +188,11 @@
     send_part()
     for load in loads[2:]:
         load.wait()
-    lax.fori_loop(0, KV_HEADS, own, 0)
+    lax.fori_loop(0, KV_HEADS - 1, own, 0)
     shared = 0
     for j in range(PLANES):
+        if j == 1:
+            lax.fori_loop(KV_HEADS - 1, KV_HEADS, own, 0)
         send_plane(j)
         if j >= 2 and j % 2 == 0 and shared < CHUNKS[0][1]:
             share_plane(shared)
@@ -209,14 +211,18 @@
             keys = kv_ref[begin:end, :, :, 0, :, lanes].reshape(count, HEAD)
             values = kv_ref[begin:end, :, :, 1, :, lanes].reshape(count, HEAD)
             attend(h, keys, values, False, last, *refs)
-            if last:
-                columns = pl.ds(pl.multiple_of(h * GROUPS * HEAD, GROUPS * HEAD), GROUPS * HEAD)
-                pltpu.make_async_copy(
-                    out_ref.at[:, columns], out_hbm.at[:, columns], store_sems.at[h]
-                ).start()
-            elif coming >= KV_HEADS:
-                share_plane(end + h)
-            else:
+            if coming >= KV_HEADS:
+
+                @pl.when(h == 1)
+                def _():
+                    share_plane(end)
+                    share_plane(end + 1)
+
+                @pl.when(h == 2)
+                def _():
+                    share_plane(end + 2)
+                    share_plane(end + 3)
+            elif coming:
 
                 @pl.when(h < coming)
                 def _():
@@ -232,11 +238,6 @@
         wait_part(j, part_send)
         wait_plane(j, plane_send)
         core_copy(j).wait_send()
-    for h in range(KV_HEADS):
-        columns = pl.ds(h * GROUPS * HEAD, GROUPS * HEAD)
-        pltpu.make_async_copy(
-            out_ref.at[:, columns], out_hbm.at[:, columns], store_sems.at[h]
-        ).wait()
 
 
 def shards(queries, resp_keys, resp_values, lengths, prefix_keys, prefix_values):
@@ -247,7 +248,7 @@
         kernel,
         out_shape=pltpu.VMEM(queries.shape, bf16),
         in_specs=[hbm] * 6,
-        out_specs=hbm,
+        out_specs=pl.BlockSpec(memory_space=pltpu.VMEM),
         scratch_shapes=[
             pltpu.SMEM(lengths.shape, jnp.int32),
             pltpu.VMEM(queries.shape, bf16),
@@ -255,13 +256,11 @@
             pltpu.VMEM(resp_values.shape, bf16),
             pltpu.VMEM(prefix_keys.shape, bf16),
             pltpu.VMEM(prefix_values.shape, bf16),
-            pltpu.VMEM(queries.shape, bf16),
             pltpu.VMEM((heads, ROWS, 2 * HEAD), f32),
             pltpu.VMEM((heads, ROWS, HEAD), f32),
             pltpu.VMEM((PLANES, RING, 2, 16, HEAD), bf16),
             pltpu.VMEM((PLANES, 2, RING, 2, 16, KV_HEADS * HEAD), bf16),
             pltpu.SemaphoreType.DMA((6,)),
-            pltpu.SemaphoreType.DMA((KV_HEADS,)),
         ]
         + [pltpu.SemaphoreType.DMA((PLANES,))] * 6,
         compiler_params=pltpu.CompilerParams(

time: 40.9 us -> 40.2 us (0.983)
  Pallas kernels: 38.8 us -> 38.1 us
    pallas_call x1, Pallas kernels: 38.8 us -> 38.1 us  [shards(): pl.pallas_call(kernel, out_shape=pltpu.VMEM(queries.shape, bf16), in_spec...]
where the time goes in v3:
time: 40.2 us; the launch traced here: 40.1 us
  Pallas kernels  38.1 us (95%)
  local copies, waits for them, and re-layouts  1.32 us (3%)
  between operations  0.66 us (2%)
    pallas_call x1, Pallas kernels, shards(): pl.pallas_call(kernel, out_shape=pltpu.VMEM(queries.shape, bf16), in_spec...  38.1 us
    unnamed x1, local copies, waits for them, and re-layouts  1.32 us

profile of v3, /device:TPU:1, one launch (start us, length us, event | category | flops | bytes accessed | tf_op | source)
XLA Modules:
  0.0 40.1 jit_solution(17376401805424548674)
XLA Ops:
  0.7 38.1 %attend_and_gather.1 = bf16[256,4096]{1,0:T(8,128)(2,1)S(1)} custom-call(bf16[256,4096]{1,0:T(8,128)(2,1)} %q_hbm.1, bf16[256,512]{1,0:T(8,128)(2,1)} %ok_hbm.1, bf16[256,512]{1,0:T(8,128)(2,1)} %ov_hbm.1, s32[1]{0:T(128)S(6)} %copy.9.len_hbm, bf16[4,512]{1,0:T(4,128)(2,1)} %pk_hbm.1, bf16[4,512]{1,0:T(4,128)(2,1)} %pv_hbm.1), custom_call_target="tpu_custom_call" | custom-call | tf_op jit(solution)/shard_map/attend_and_gather/pallas_call | solution.py:247
  38.8 1.3 %copy.8 = bf16[256,4096]{1,0:T(8,128)(2,1)} copy(bf16[256,4096]{1,0:T(8,128)(2,1)S(1)} %attend_and_gather.1) | data formatting | bytes 4194304

commit v4 on v3

--- a/solution.py
+++ b/solution.py
@@ -22,6 +22,7 @@
 RING = len(RING_OFFSETS)
 
 CHUNKS = ((0, 2), (2, 8))
+LAST_HEADS = 2
 
 
 def device(x, y, z, core):
@@ -36,19 +37,18 @@
     return pl.ds(pl.multiple_of(index * HEAD, HEAD), HEAD)
 
 
-def attend(h, keys, values, first, last, len_ref, q_ref, out_ref, acc_ref, max_ref):
-    ones = jnp.ones((values.shape[0], HEAD), jnp.bfloat16)
-    values_and_ones = jnp.concatenate([values, ones], axis=1)
-
-    def scores_of(g):
-        return matmul(q_ref[:, head_lanes(h * GROUPS + g)], keys, NT)
-
-    def weigh(g, scores):
-        head = h * GROUPS + g
+def attend(blocks, first, last, len_ref, q_ref, out_ref, acc_ref, max_ref):
+    count = blocks[0][1].shape[0]
+    ones = jnp.ones((count, HEAD), jnp.bfloat16)
+    heads = [(h * GROUPS + g, n) for n, (h, _, _) in enumerate(blocks) for g in range(GROUPS)]
+
+    def scores_of(head, n):
+        return matmul(q_ref[:, head_lanes(head)], blocks[n][1], NT)
+
+    def weigh(head, scores):
         if first:
-            own = keys.shape[0]
-            column = lax.broadcasted_iota(jnp.int32, (ROWS, own), 1)
-            row = lax.broadcasted_iota(jnp.int32, (ROWS, own), 0)
+            column = lax.broadcasted_iota(jnp.int32, (ROWS, count), 1)
+            row = lax.broadcasted_iota(jnp.int32, (ROWS, count), 0)
             scores = jnp.where(column <= row, scores, -1e30)
         top = jnp.max(scores, axis=1, keepdims=True) * BASE2_SCALE
         top = jnp.broadcast_to(top, (ROWS, HEAD))
@@ -65,9 +65,8 @@
         ]
         return jnp.concatenate(parts, axis=1), factor
 
-    def mix(g, weights, factor):
-        head = h * GROUPS + g
-        total = matmul(weights, values_and_ones, NN)
+    def mix(head, n, weights, factor):
+        total = matmul(weights, jnp.concatenate([blocks[n][2], ones], axis=1), NN)
         if not first:
             total = acc_ref[head] * jnp.concatenate([factor, factor], axis=1) + total
         if not last:
@@ -78,12 +77,12 @@
         result = jnp.where(position < len_ref[0], result, 0.0)
         out_ref[:, head_lanes(head)] = result.astype(jnp.bfloat16)
 
-    following = scores_of(0)
-    for g in range(GROUPS):
+    following = scores_of(*heads[0])
+    for index, (head, n) in enumerate(heads):
         current = following
-        if g + 1 < GROUPS:
-            following = scores_of(g + 1)
-        mix(g, *weigh(g, current))
+        if index + 1 < len(heads):
+            following = scores_of(*heads[index + 1])
+        mix(head, n, *weigh(head, current))
 
 
 def kernel(
@@ -181,7 +180,7 @@
 
     def own(h, carry):
         lanes = head_lanes(h)
-        attend(h, ok_ref[:, lanes], ov_ref[:, lanes], True, False, *refs)
+        attend([(h, ok_ref[:, lanes], ov_ref[:, lanes])], True, False, *refs)
         return carry
 
     pl.semaphore_wait(barrier, len(first_peers) + RING - 1 + 1)
@@ -205,12 +204,18 @@
         for j in range(begin, end):
             core_copy(j).wait_recv()
 
-        def prompt(h, carry, begin=begin, end=end, last=last, coming=coming):
-            lanes = head_lanes(h)
+        width = LAST_HEADS if last else 1
+
+        def prompt(step, carry, begin=begin, end=end, last=last, coming=coming, width=width):
             count = (end - begin) * 128
-            keys = kv_ref[begin:end, :, :, 0, :, lanes].reshape(count, HEAD)
-            values = kv_ref[begin:end, :, :, 1, :, lanes].reshape(count, HEAD)
-            attend(h, keys, values, False, last, *refs)
+            blocks = []
+            for n in range(width):
+                h = step * width + n
+                lanes = head_lanes(h)
+                keys = kv_ref[begin:end, :, :, 0, :, lanes].reshape(count, HEAD)
+                values = kv_ref[begin:end, :, :, 1, :, lanes].reshape(count, HEAD)
+                blocks.append((h, keys, values))
+            attend(blocks, False, last, *refs)
             if coming >= KV_HEADS:
 
                 @pl.when(h == 1)
@@ -230,7 +235,7 @@
 
             return carry
 
-        lax.fori_loop(0, KV_HEADS, prompt, 0)
+        lax.fori_loop(0, KV_HEADS // width, prompt, 0)
         for j in range(end + KV_HEADS, end + coming):
             share_plane(j)
 

time: 40.2 us -> 39.6 us (0.985)
  Pallas kernels: 38.1 us -> 37.5 us
    pallas_call x1, Pallas kernels: 38.1 us -> 37.5 us  [shards(): pl.pallas_call(kernel, out_shape=pltpu.VMEM(queries.shape, bf16), in_spec...]
where the time goes in v4:
time: 39.6 us; the launch traced here: 39.5 us
  Pallas kernels  37.5 us (95%)
  local copies, waits for them, and re-layouts  1.32 us (3%)
  between operations  0.66 us (2%)
    pallas_call x1, Pallas kernels, shards(): pl.pallas_call(kernel, out_shape=pltpu.VMEM(queries.shape, bf16), in_spec...  37.5 us
    unnamed x1, local copies, waits for them, and re-layouts  1.32 us

profile of v4, /device:TPU:1, one launch (start us, length us, event | category | flops | bytes accessed | tf_op | source)
XLA Modules:
  0.0 39.5 jit_solution(8471735286245223055)
XLA Ops:
  0.7 37.5 %attend_and_gather.1 = bf16[256,4096]{1,0:T(8,128)(2,1)S(1)} custom-call(bf16[256,4096]{1,0:T(8,128)(2,1)} %q_hbm.1, bf16[256,512]{1,0:T(8,128)(2,1)} %ok_hbm.1, bf16[256,512]{1,0:T(8,128)(2,1)} %ov_hbm.1, s32[1]{0:T(128)S(6)} %copy.9.len_hbm, bf16[4,512]{1,0:T(4,128)(2,1)} %pk_hbm.1, bf16[4,512]{1,0:T(4,128)(2,1)} %pv_hbm.1), custom_call_target="tpu_custom_call" | custom-call | tf_op jit(solution)/shard_map/attend_and_gather/pallas_call | solution.py:252
  38.2 1.3 %copy.8 = bf16[256,4096]{1,0:T(8,128)(2,1)} copy(bf16[256,4096]{1,0:T(8,128)(2,1)S(1)} %attend_and_gather.1) | data formatting | bytes 4194304
